TPU v7x, 128 devices: a whole 4x4x4 slice. The times are simulated.
128 devices in a mesh: rows: 32 (over z, y, core), vecs: 4 (over x).
Axes of the slice: x: 4, y: 4, z: 4, core: 2. Of those that a mesh axis runs over, the one named last changes fastest.
Arguments:
- vectors: bfloat16 [131072, 1024], P('rows', 'vecs'), may hold values from -6 to 6, as said below
- blocks: bfloat16 [1024, 5, 128, 128], P('rows'), may hold values from -0.25 to 0.25
- columns: int32 [1024, 5], P('rows'), may hold values from 0 to 1023, as said below
Outputs:
- basis: float32 [131072, 1024], P('rows', 'vecs')
Inputs may be any that keep to these rules, and one draw needn't show every extreme that they name: Each block row i names 5 block columns of the form i + d clipped to 0 .. 1023, with distinct d in -8 .. 8; near the grid's ends some may repeat. `vectors`: entries of order one.
All inputs are finite; a program needn't handle non-finite values.
Results may differ from a plain program's by a relative error of at most 0.0075.
Values may be sent and summed in bfloat16 or wider, within the bound.
No kernel may reach another device: no remote copies, remote signals or barrier semaphores. Data moves between devices by JAX's collectives and lax.ppermute only.
A program may use at most 128 MiB of HBM per device.

v0:
```python
import jax
import jax.numpy as jnp
from jax import lax
from jax.sharding import PartitionSpec as P

DEGREE = 4
filter_center = 0.25
filter_radius = 1.25


def with_halo(shard, sides, width):
    for axis, dim in sides:
        count, length = (lax.axis_size(axis), shard.shape[dim])
        up = [(i, (i + 1) % count) for i in range(count - 1)]
        down = [(j, i) for i, j in up]
        last = lax.slice_in_dim(shard, length - width, length, axis=dim)
        first = lax.slice_in_dim(shard, 0, width, axis=dim)
        before = lax.ppermute(last, axis, up)
        after = lax.ppermute(first, axis, down)
        shard = jnp.concatenate([before, shard, after], axis=dim)
    return shard


def product(vec_bf, blocks, local_index):
    block_rows = blocks.shape[0]
    size_b = blocks.shape[2]
    width = vec_bf.shape[1]
    reach = block_rows // 4
    padded = with_halo(vec_bf, (("rows", 0),), reach * size_b)
    stacked = padded.reshape(block_rows + 2 * reach, size_b, width)
    picked = stacked[local_index]
    result = jnp.einsum("rjab,rjbk->rak", blocks, picked, preferred_element_type=jnp.float32)
    return result.reshape(block_rows * size_b, width)


def split_apply(left_bf, factor):
    factor_high = factor.astype(jnp.bfloat16)
    factor_low = (factor - factor_high.astype(jnp.float32)).astype(jnp.bfloat16)
    first = jnp.dot(left_bf, factor_high.T, preferred_element_type=jnp.float32)
    second = jnp.dot(left_bf, factor_low.T, preferred_element_type=jnp.float32)
    return first + second


def shards(vectors, blocks, columns):
    block_rows = blocks.shape[0]
    reach = block_rows // 4
    first_row = lax.axis_index("rows") * block_rows
    local_index = columns - first_row + reach
    total_rows = vectors.shape[0] * lax.axis_size("rows")
    older = vectors.astype(jnp.float32)
    current = (product(vectors, blocks, local_index) - filter_center * older) / filter_radius
    for iteration in range(1, DEGREE):
        rounded = current.astype(jnp.bfloat16)
        newer = (
            2.0 * (product(rounded, blocks, local_index) - filter_center * current) / filter_radius
            - older
        )
        older = current
        current = newer
    final = current.astype(jnp.bfloat16)
    panel_width = final.shape[1]
    full_width = panel_width * lax.axis_size("vecs")
    identity = jnp.eye(full_width, dtype=jnp.float32)
    whole_block = lax.all_gather(final, "vecs", axis=1, tiled=True)
    panel = jnp.dot(final.T, whole_block, preferred_element_type=jnp.float32)
    summed = lax.psum(panel, "rows")
    gram_matrix = lax.all_gather(summed, "vecs", axis=0, tiled=True) / total_rows
    lower = jnp.linalg.cholesky(gram_matrix)
    inverse = lax.linalg.triangular_solve(lower, identity, left_side=True, lower=True)
    own_rows = lax.dynamic_slice_in_dim(
        inverse, lax.axis_index("vecs") * panel_width, panel_width, 0
    )
    return split_apply(whole_block, own_rows)


def solution(mesh):
    in_specs = (P("rows", "vecs"), P("rows", None, None, None), P("rows", None))
    out_specs = P("rows", "vecs")
    return jax.shard_map(shards, mesh=mesh, in_specs=in_specs, out_specs=out_specs, check_vma=False)
```

profile of v0, /device:TPU:1, one launch (start us, length us, event | category | flops | bytes accessed | tf_op | source)
XLA Modules:
  0.0 772.8 jit_solution(1005979501189157616)
XLA Ops:
  25.1 7.6 gather_fusion
  32.7 7.5 fusion.88
  56.7 9.5 %gather_fusion.1 = bf16[160,128,256]{2,1,0:T(8,128)(2,1)} fusion(bf16[48,128,256]{2,1,0:T(8,128)(2,1)} %bitcast.194, s32[1024]{0:T(1024)S(1)} %pad_clamp_fusion), kind=kCustom, calls=%fused_computation.1 | custom fusion | bytes 20972160 | tf_op jit(solution)/shard_map/gather | solution.py:31
  66.2 7.5 fusion.89
  90.1 9.5 %gather_fusion.2 = bf16[160,128,256]{2,1,0:T(8,128)(2,1)} fusion(bf16[48,128,256]{2,1,0:T(8,128)(2,1)} %bitcast.195, s32[1024]{0:T(1024)S(1)} %pad_clamp_fusion), kind=kCustom, calls=%fused_computation.2 | custom fusion | bytes 20972160 | tf_op jit(solution)/shard_map/gather | solution.py:31
  99.6 7.5 fusion.90
  118.3 6.1 collective-permute-done.7
  126.3 9.5 %gather_fusion.3 = bf16[160,128,256]{2,1,0:T(8,128)(2,1)} fusion(bf16[48,128,256]{2,1,0:T(8,128)(2,1)} %bitcast.193, s32[1024]{0:T(1024)S(1)} %pad_clamp_fusion), kind=kCustom, calls=%fused_computation.3 | custom fusion | bytes 20972160 | tf_op jit(solution)/shard_map/gather | solution.py:31
  135.7 7.5 fusion.91
  149.4 94.6 %all-gather.3.cloned.1.call-done = bf16[4096,1024]{1,0:T(8,128)(2,1)} async-done(((bf16[4096,256]{1,0:T(8,128)(2,1)}), bf16[4096,1024]{1,0:T(8,128)(2,1)}) %all-gather.3.cloned.1.call-update) | async-done | bytes 8388624 | tf_op jit(solution)/shard_map/all_gather | solution.py:64
  244.0 8.4 %fusion.87 = f32[256,1024]{0,1:T(8,128)} fusion(bf16[4096,256]{1,0:T(8,128)(2,1)} %fusion.3, bf16[4096,1024]{1,0:T(8,128)(2,1)} %all-gather.3.cloned.1.call-done), kind=kOutput, calls=%fused_computation.195 | convolution fusion | flops 2147483648 | bytes 11534336 | tf_op jit(solution)/shard_map/dot_general | solution.py:65
  252.5 106.3 %all-reduce.3.cloned.1.call-done = f32[256,1024]{0,1:T(8,128)} async-done(((f32[256,1024]{0,1:T(8,128)}), f32[256,1024]{0,1:T(8,128)}) %all-reduce.3.cloned.1.call-update) | async-done | bytes 1048592 | tf_op jit(solution)/shard_map/psum | solution.py:66
  361.7 46.9 %all-gather.5.cloned.1.call-done = f32[1024,1024]{0,1:T(8,128)} async-done(((f32[256,1024]{0,1:T(8,128)}), f32[1024,1024]{0,1:T(8,128)}) %all-gather.5.cloned.1.call-update) | async-done | bytes 4194320 | tf_op jit(solution)/shard_map/all_gather | solution.py:67
  408.6 5.0 broadcast_multiply_fusion
  413.6 5.5 copy.8
  425.5 11.7 %cholesky.223 = f32[128,128]{1,0:T(8,128)S(1)} custom-call(f32[128,128]{1,0:T(8,128)S(1)} %cholesky.580), custom_call_target="Cholesky" | custom-call | tf_op jit(solution)/shard_map/jit(cholesky)/cholesky | solution.py:68
  437.3 9.8 %custom-call.62 = f32[1,128,128]{1,2,0:T(8,128)S(1)} custom-call(f32[1,128,128]{2,1,0:T(8,128)S(1)} %get-tuple-element.77), custom_call_target="InvertDiagBlocksLowerTriangular" | custom-call | tf_op jit(solution)/shard_map/jit(cholesky)/cholesky | solution.py:68
  453.5 11.9 %cholesky.244 = f32[128,128]{1,0:T(8,128)S(1)} custom-call(f32[128,128]{1,0:T(8,128)S(1)} %cholesky.584), custom_call_target="Cholesky" | custom-call | tf_op jit(solution)/shard_map/jit(cholesky)/cholesky | solution.py:68
  466.1 9.8 %custom-call.63 = f32[1,128,128]{1,2,0:T(8,128)S(1)} custom-call(f32[1,128,128]{2,1,0:T(8,128)S(1)} %get-tuple-element.74), custom_call_target="InvertDiagBlocksLowerTriangular" | custom-call | tf_op jit(solution)/shard_map/jit(cholesky)/cholesky | solution.py:68
  479.2 11.7 %cholesky.468 = f32[128,128]{1,0:T(8,128)S(1)} custom-call(f32[128,128]{1,0:T(8,128)S(1)} %cholesky.589), custom_call_target="Cholesky" | custom-call | tf_op jit(solution)/shard_map/jit(cholesky)/cholesky | solution.py:68
  492.2 9.8 %custom-call.64 = f32[1,128,128]{1,2,0:T(8,128)S(1)} custom-call(f32[1,128,128]{2,1,0:T(8,128)S(1)} %get-tuple-element.71), custom_call_target="InvertDiagBlocksLowerTriangular" | custom-call | tf_op jit(solution)/shard_map/jit(cholesky)/cholesky | solution.py:68
  505.5 12.1 %cholesky.487 = f32[128,128]{1,0:T(8,128)S(1)} custom-call(f32[128,128]{1,0:T(8,128)S(1)} %cholesky.594), custom_call_target="Cholesky" | custom-call | tf_op jit(solution)/shard_map/jit(cholesky)/cholesky | solution.py:68
  519.0 9.8 %custom-call.65 = f32[1,128,128]{1,2,0:T(8,128)S(1)} custom-call(f32[1,128,128]{2,1,0:T(8,128)S(1)} %get-tuple-element.68), custom_call_target="InvertDiagBlocksLowerTriangular" | custom-call | tf_op jit(solution)/shard_map/jit(cholesky)/cholesky | solution.py:68
  532.2 11.7 %cholesky.506 = f32[128,128]{1,0:T(8,128)S(1)} custom-call(f32[128,128]{1,0:T(8,128)S(1)} %cholesky.599), custom_call_target="Cholesky" | custom-call | tf_op jit(solution)/shard_map/jit(cholesky)/cholesky | solution.py:68
  545.2 10.0 %custom-call.66 = f32[1,128,128]{1,2,0:T(8,128)S(1)} custom-call(f32[1,128,128]{2,1,0:T(8,128)S(1)} %get-tuple-element.65), custom_call_target="InvertDiagBlocksLowerTriangular" | custom-call | tf_op jit(solution)/shard_map/jit(cholesky)/cholesky | solution.py:68
  558.5 11.7 %cholesky.526 = f32[128,128]{1,0:T(8,128)S(1)} custom-call(f32[128,128]{1,0:T(8,128)S(1)} %cholesky.604), custom_call_target="Cholesky" | custom-call | tf_op jit(solution)/shard_map/jit(cholesky)/cholesky | solution.py:68
  571.5 9.8 %custom-call.67 = f32[1,128,128]{1,2,0:T(8,128)S(1)} custom-call(f32[1,128,128]{2,1,0:T(8,128)S(1)} %get-tuple-element.62), custom_call_target="InvertDiagBlocksLowerTriangular" | custom-call | tf_op jit(solution)/shard_map/jit(cholesky)/cholesky | solution.py:68
  584.2 11.9 %cholesky.546 = f32[128,128]{1,0:T(8,128)S(1)} custom-call(f32[128,128]{1,0:T(8,128)S(1)} %cholesky.609), custom_call_target="Cholesky" | custom-call | tf_op jit(solution)/shard_map/jit(cholesky)/cholesky | solution.py:68
  597.5 9.8 %custom-call.68 = f32[1,128,128]{1,2,0:T(8,128)S(1)} custom-call(f32[1,128,128]{2,1,0:T(8,128)S(1)} %get-tuple-element.59), custom_call_target="InvertDiagBlocksLowerTriangular" | custom-call | tf_op jit(solution)/shard_map/jit(cholesky)/cholesky | solution.py:68
  609.9 11.7 %cholesky.564 = f32[128,128]{1,0:T(8,128)S(1)} custom-call(f32[128,128]{1,0:T(8,128)S(1)} %convolution_subtract_fusion.11), custom_call_target="Cholesky" | custom-call | tf_op jit(solution)/shard_map/jit(cholesky)/cholesky | solution.py:68
  633.4 23.9 %while.1 = (s32[]{:T(128)}, f32[1024,1024]{1,0:T(8,128)}, s32[8,2]{0,1:T(2,128)S(1)}, f32[8,128,128]{2,1,0:T(8,128)S(1)}, s32[]{:T(128)}) while((s32[]{:T(128)}, f32[1024,1024]{1,0:T(8,128)}, s32[8,2]{0,1:T(2,128)S(1)}, f32[8,128,128]{2,1,0:T(8,128)S(1)}, s32[]{:T(128)}) %tuple.61), condition=%wide.while_cond, body=%wide.while_body.sunk | while | flops 2 | bytes 131189 | solution.py:69
  657.3 79.0 %custom-call.69 = f32[8,128,128]{1,2,0:T(8,128)S(1)} custom-call(f32[8,128,128]{2,1,0:T(8,128)S(1)} %get-tuple-element.12), custom_call_target="InvertDiagBlocksLowerTriangular" | custom-call | tf_op jit(solution)/shard_map/triangular_solve | solution.py:69
  (153 shorter events, 172.5 us)
Async XLA Ops:
  6.5 237.5 %all-gather.3.cloned.1.call-start = ((), (), s32[]{:S(2)}) async-start(), calls=%async_computation | async-start | bytes 10485760 | tf_op jit(solution)/shard_map/all_gather | solution.py:64
  7.8 10.7 %collective-permute-start = (bf16[1024,256]{1,0:T(8,128)(2,1)S(1)}, bf16[1024,256]{1,0:T(8,128)(2,1)S(1)}, u32[]{:S(2)}, u32[]{:S(2)}) collective-permute-start(bf16[1024,256]{1,0:T(8,128)(2,1)S(1)} %get-tuple-element.29), channel_id=1, source_target_pairs={{0,4},{4,8},{8,12},{12,16},{16,20},{20,24},{24,28},{28,32},{32,36}... | collective-permute-start | bytes 1572872 | tf_op jit(solution)/shard_map/ppermute | solution.py:18
  12.4 10.6 %collective-permute-start.1 = (bf16[1024,256]{1,0:T(8,128)(2,1)S(1)}, bf16[1024,256]{1,0:T(8,128)(2,1)}, u32[]{:S(2)}, u32[]{:S(2)}) collective-permute-start(bf16[1024,256]{1,0:T(8,128)(2,1)S(1)} %get-tuple-element.30), channel_id=1, source_target_pairs={{4,0},{8,4},{12,8},{16,12},{20,16},{24,20},{28,24},{32,28},{36,32}... | collective-permute-start | bytes 1572872 | tf_op jit(solution)/shard_map/ppermute | solution.py:19
  18.5 0.8 copy-start.12
  32.7 7.5 copy-start.7
  40.3 2.0 copy-start
  42.4 8.0 %collective-permute-start.2 = (bf16[1024,256]{1,0:T(8,128)(2,1)S(1)}, bf16[1024,256]{1,0:T(8,128)(2,1)S(1)}, u32[]{:S(2)}, u32[]{:S(2)}) collective-permute-start(bf16[1024,256]{1,0:T(8,128)(2,1)S(1)} %get-tuple-element.27), channel_id=1, source_target_pairs={{0,4},{4,8},{8,12},{12,16},{16,20},{20,24},{24,28},{28,32},{32,36}... | collective-permute-start | bytes 1572872 | tf_op jit(solution)/shard_map/ppermute | solution.py:18
  44.3 10.5 %collective-permute-start.3 = (bf16[1024,256]{1,0:T(8,128)(2,1)S(1)}, bf16[1024,256]{1,0:T(8,128)(2,1)S(1)}, u32[]{:S(2)}, u32[]{:S(2)}) collective-permute-start(bf16[1024,256]{1,0:T(8,128)(2,1)S(1)} %get-tuple-element.28), channel_id=1, source_target_pairs={{4,0},{8,4},{12,8},{16,12},{20,16},{24,20},{28,24},{32,28},{36,32}... | collective-permute-start | bytes 1572872 | tf_op jit(solution)/shard_map/ppermute | solution.py:19
  66.2 7.5 copy-start.1
  73.7 2.1 copy-start.4
  75.9 8.0 %collective-permute-start.4 = (bf16[1024,256]{1,0:T(8,128)(2,1)S(1)}, bf16[1024,256]{1,0:T(8,128)(2,1)S(1)}, u32[]{:S(2)}, u32[]{:S(2)}) collective-permute-start(bf16[1024,256]{1,0:T(8,128)(2,1)S(1)} %get-tuple-element.25), channel_id=1, source_target_pairs={{0,4},{4,8},{8,12},{12,16},{16,20},{20,24},{24,28},{28,32},{32,36}... | collective-permute-start | bytes 1572872 | tf_op jit(solution)/shard_map/ppermute | solution.py:18
  77.8 10.5 %collective-permute-start.5 = (bf16[1024,256]{1,0:T(8,128)(2,1)S(1)}, bf16[1024,256]{1,0:T(8,128)(2,1)S(1)}, u32[]{:S(2)}, u32[]{:S(2)}) collective-permute-start(bf16[1024,256]{1,0:T(8,128)(2,1)S(1)} %get-tuple-element.26), channel_id=1, source_target_pairs={{4,0},{8,4},{12,8},{16,12},{20,16},{24,20},{28,24},{32,28},{36,32}... | collective-permute-start | bytes 1572872 | tf_op jit(solution)/shard_map/ppermute | solution.py:19
  99.6 7.5 copy-start.2
  99.6 8.0 %copy-start.5 = (f32[32,256,128,1]{1,2,3,0:T(8,128)S(1)}, f32[32,256,128,1]{1,2,3,0:T(8,128)}, u32[]{:S(2)}) copy-start(f32[32,256,128,1]{1,2,3,0:T(8,128)} %copy-done.4) | copy-start | bytes 12582916
  107.6 2.6 copy-start.8
  110.3 8.0 %collective-permute-start.6 = (bf16[1024,256]{1,0:T(8,128)(2,1)S(1)}, bf16[1024,256]{1,0:T(8,128)(2,1)S(1)}, u32[]{:S(2)}, u32[]{:S(2)}) collective-permute-start(bf16[1024,256]{1,0:T(8,128)(2,1)S(1)} %get-tuple-element.23), channel_id=1, source_target_pairs={{0,4},{4,8},{8,12},{12,16},{16,20},{20,24},{24,28},{28,32},{32,36}... | collective-permute-start | bytes 1572872 | tf_op jit(solution)/shard_map/ppermute | solution.py:18
  112.2 12.2 %collective-permute-start.7 = (bf16[1024,256]{1,0:T(8,128)(2,1)S(1)}, bf16[1024,256]{1,0:T(8,128)(2,1)S(1)}, u32[]{:S(2)}, u32[]{:S(2)}) collective-permute-start(bf16[1024,256]{1,0:T(8,128)(2,1)S(1)} %get-tuple-element.24), channel_id=1, source_target_pairs={{4,0},{8,4},{12,8},{16,12},{20,16},{24,20},{28,24},{32,28},{36,32}... | collective-permute-start | bytes 1572872 | tf_op jit(solution)/shard_map/ppermute | solution.py:19
  135.7 7.5 copy-start.3
  135.7 8.0 %copy-start.6 = (f32[32,256,128,1]{1,2,3,0:T(8,128)S(1)}, f32[32,256,128,1]{1,2,3,0:T(8,128)}, u32[]{:S(2)}) copy-start(f32[32,256,128,1]{1,2,3,0:T(8,128)} %copy-done.4) | copy-start | bytes 12582916
  135.7 9.2 %copy-start.9 = (f32[32,256,128,1]{1,2,3,0:T(8,128)S(1)}, f32[32,256,128,1]{1,2,3,0:T(8,128)}, u32[]{:S(2)}) copy-start(f32[32,256,128,1]{1,2,3,0:T(8,128)} %copy-done.8) | copy-start | bytes 12582916
  149.3 209.5 %all-reduce.3.cloned.1.call-start = ((), (), s32[]{:S(2)}) async-start(), calls=%async_computation.1 | async-start | bytes 2097152 | tf_op jit(solution)/shard_map/psum | solution.py:66
  252.5 156.1 %all-gather.5.cloned.1.call-start = ((), (), s32[]{:S(2)}) async-start(), calls=%async_computation.2 | async-start | bytes 5242880 | tf_op jit(solution)/shard_map/all_gather | solution.py:67
  423.6 1.9 copy-start.11
  736.3 3.2 copy-start.10
  747.7 11.2 %slice-start = ((s8[8388608]{0:T(1024)(128)(4,1)}), s8[4194304]{0:T(1024)(128)(4,1)S(1)}, s32[]{:S(2)}) async-start(s8[8388608]{0:T(1024)(128)(4,1)} %bitcast.197), calls=%async_computation.3 | async-start | bytes 8388608
  751.2 7.7 slice-start.1
Sparse Core Ops, SparseCore 0:
  149.5 94.5 all-gather.2
  252.6 106.2 all-reduce.2
  360.6 47.9 all-gather.4
where the time goes:
time: 782 us; the launch traced here: 773 us
  other arithmetic  287 us (37%)
  waiting for transfers between devices  280 us (36%)
  matrix products  91 us (12%)
  local copies, waits for them, and re-layouts  75.8 us (10%)
  starting transfers between devices  20.1 us (3%)
  between operations  18.8 us (2%)
    another operation x30, other arithmetic, shards(): lower = jnp.linalg.cholesky(gram_matrix)  172 us
    psum x1, waiting for transfers between devices, shards(): summed = lax.psum(panel, 'rows')  106 us
    all_gather x1, waiting for transfers between devices, shards(): whole_block = lax.all_gather(final, 'vecs', axis=1, tiled=True)  94.6 us
    another operation x3, other arithmetic, shards(): lax.linalg.triangular_solve(lower, identity, left_side=True, lower=True)  83.9 us
    all_gather x1, waiting for transfers between devices, shards(): lax.all_gather(summed, 'vecs', axis=0, tiled=True) / total_rows  46.9 us
    gather x4, local copies, waits for them, and re-layouts, product(): picked = stacked[local_index]  36.1 us
    dot_general x4, matrix products, product(): jnp.einsum('rjab,rjbk->rak', blocks, picked, preferred_element_type=jnp.f...  30.1 us
    another operation x24, local copies, waits for them, and re-layouts  23.8 us
  transfers between devices with their start and end apart: 11, of which 11 were waited for; matrix products, arithmetic and copies ran while one was open for 0% of the time, Pallas kernels for 0%

commit v1 on v0

--- a/solution.py
+++ b/solution.py
@@ -63,7 +63,7 @@
     identity = jnp.eye(full_width, dtype=jnp.float32)
     whole_block = lax.all_gather(final, "vecs", axis=1, tiled=True)
     panel = jnp.dot(final.T, whole_block, preferred_element_type=jnp.float32)
-    summed = lax.psum(panel, "rows")
+    summed = jnp.sum(lax.all_gather(panel, "rows"), axis=0)
     gram_matrix = lax.all_gather(summed, "vecs", axis=0, tiled=True) / total_rows
     lower = jnp.linalg.cholesky(gram_matrix)
     inverse = lax.linalg.triangular_solve(lower, identity, left_side=True, lower=True)

time: 782 us -> 800 us (1.023)
  other arithmetic: 287 us -> 299 us
    all_gather x0 -> x1, waiting for transfers between devices: none -> 116 us  [shards(): summed = jnp.sum(lax.all_gather(panel, 'rows'), axis=0)]
    psum x1 -> x0, waiting for transfers between devices: 106 us -> none  [shards(): summed = lax.psum(panel, 'rows')]
    reduce_sum x0 -> x1, other arithmetic: none -> 11.8 us  [shards(): summed = jnp.sum(lax.all_gather(panel, 'rows'), axis=0)]
where the time goes in v1:
time: 800 us; the launch traced here: 791 us
  other arithmetic  299 us (37%)
  waiting for transfers between devices  287 us (36%)
  matrix products  89.9 us (11%)
  local copies, waits for them, and re-layouts  76.1 us (10%)
  starting transfers between devices  20.1 us (3%)
  between operations  19 us (2%)
    another operation x30, other arithmetic, shards(): lower = jnp.linalg.cholesky(gram_matrix)  173 us
    all_gather x1, waiting for transfers between devices, shards(): summed = jnp.sum(lax.all_gather(panel, 'rows'), axis=0)  116 us
    all_gather x1, waiting for transfers between devices, shards(): whole_block = lax.all_gather(final, 'vecs', axis=1, tiled=True)  94.6 us
    another operation x3, other arithmetic, shards(): lax.linalg.triangular_solve(lower, identity, left_side=True, lower=True)  83.9 us
    all_gather x1, waiting for transfers between devices, shards(): lax.all_gather(summed, 'vecs', axis=0, tiled=True) / total_rows  44.3 us
    gather x4, local copies, waits for them, and re-layouts, product(): picked = stacked[local_index]  36.1 us
    dot_general x4, matrix products, product(): jnp.einsum('rjab,rjbk->rak', blocks, picked, preferred_element_type=jnp.f...  30.1 us
    another operation x14, matrix products, shards(): lower = jnp.linalg.cholesky(gram_matrix)  22.9 us
  transfers between devices with their start and end apart: 11, of which 11 were waited for; matrix products, arithmetic and copies ran while one was open for 0% of the time, Pallas kernels for 0%

profile of v1, /device:TPU:1, one launch (start us, length us, event | category | flops | bytes accessed | tf_op | source)
XLA Modules:
  0.0 790.9 jit_solution(12371333019377978486)
XLA Ops:
  25.1 7.6 gather_fusion
  32.7 7.5 fusion.88
  56.7 9.5 %gather_fusion.1 = bf16[160,128,256]{2,1,0:T(8,128)(2,1)} fusion(bf16[48,128,256]{2,1,0:T(8,128)(2,1)} %bitcast.195, s32[1024]{0:T(1024)S(1)} %pad_clamp_fusion), kind=kCustom, calls=%fused_computation.1 | custom fusion | bytes 20972160 | tf_op jit(solution)/shard_map/gather | solution.py:31
  66.2 7.5 fusion.89
  90.1 9.5 %gather_fusion.2 = bf16[160,128,256]{2,1,0:T(8,128)(2,1)} fusion(bf16[48,128,256]{2,1,0:T(8,128)(2,1)} %bitcast.196, s32[1024]{0:T(1024)S(1)} %pad_clamp_fusion), kind=kCustom, calls=%fused_computation.2 | custom fusion | bytes 20972160 | tf_op jit(solution)/shard_map/gather | solution.py:31
  99.6 7.5 fusion.90
  118.3 6.1 collective-permute-done.7
  126.3 9.5 %gather_fusion.3 = bf16[160,128,256]{2,1,0:T(8,128)(2,1)} fusion(bf16[48,128,256]{2,1,0:T(8,128)(2,1)} %bitcast.194, s32[1024]{0:T(1024)S(1)} %pad_clamp_fusion), kind=kCustom, calls=%fused_computation.3 | custom fusion | bytes 20972160 | tf_op jit(solution)/shard_map/gather | solution.py:31
  135.7 7.5 fusion.91
  149.4 94.6 %all-gather.5.cloned.1.call-done = bf16[4096,1024]{1,0:T(8,128)(2,1)} async-done(((bf16[4096,256]{1,0:T(8,128)(2,1)}), bf16[4096,1024]{1,0:T(8,128)(2,1)}) %all-gather.5.cloned.1.call-update) | async-done | bytes 8388624 | tf_op jit(solution)/shard_map/all_gather | solution.py:64
  244.0 7.3 fusion.87
  251.4 115.8 %all-gather.9.cloned.1.call-done = f32[8192,1024]{1,0:T(8,128)} async-done(((f32[256,1024]{1,0:T(8,128)}), f32[8192,1024]{1,0:T(8,128)}) %all-gather.9.cloned.1.call-update) | async-done | bytes 33554448 | tf_op jit(solution)/shard_map/all_gather | solution.py:66
  367.2 11.8 %reduce_sum.9 = f32[256,1024]{1,0:T(8,128)S(1)} reduce(f32[32,256,1024]{2,1,0:T(8,128)} %bitcast.200, f32[]{:T(128)} %constant.301.clone.1), dimensions={0}, to_apply=%region_0.0 | reduce | flops 8126464 | bytes 34603012 | tf_op jit(solution)/shard_map/reduce_sum | solution.py:66
  383.2 44.3 %all-gather.7.cloned.1.call-done = f32[1024,1024]{0,1:T(8,128)} async-done(((f32[256,1024]{0,1:T(8,128)}), f32[1024,1024]{0,1:T(8,128)}) %all-gather.7.cloned.1.call-update) | async-done | bytes 4194320 | tf_op jit(solution)/shard_map/all_gather | solution.py:67
  432.6 5.5 copy.9
  444.6 11.7 %cholesky.223 = f32[128,128]{1,0:T(8,128)S(1)} custom-call(f32[128,128]{1,0:T(8,128)S(1)} %cholesky.580), custom_call_target="Cholesky" | custom-call | tf_op jit(solution)/shard_map/jit(cholesky)/cholesky | solution.py:68
  458.8 9.8 %custom-call.62 = f32[1,128,128]{1,2,0:T(8,128)S(1)} custom-call(f32[1,128,128]{2,1,0:T(8,128)S(1)} %get-tuple-element.77), custom_call_target="InvertDiagBlocksLowerTriangular" | custom-call | tf_op jit(solution)/shard_map/jit(cholesky)/cholesky | solution.py:68
  472.5 11.9 %cholesky.244 = f32[128,128]{1,0:T(8,128)S(1)} custom-call(f32[128,128]{1,0:T(8,128)S(1)} %cholesky.584), custom_call_target="Cholesky" | custom-call | tf_op jit(solution)/shard_map/jit(cholesky)/cholesky | solution.py:68
  485.1 9.8 %custom-call.63 = f32[1,128,128]{1,2,0:T(8,128)S(1)} custom-call(f32[1,128,128]{2,1,0:T(8,128)S(1)} %get-tuple-element.74), custom_call_target="InvertDiagBlocksLowerTriangular" | custom-call | tf_op jit(solution)/shard_map/jit(cholesky)/cholesky | solution.py:68
  498.2 11.7 %cholesky.468 = f32[128,128]{1,0:T(8,128)S(1)} custom-call(f32[128,128]{1,0:T(8,128)S(1)} %cholesky.589), custom_call_target="Cholesky" | custom-call | tf_op jit(solution)/shard_map/jit(cholesky)/cholesky | solution.py:68
  511.2 9.8 %custom-call.64 = f32[1,128,128]{1,2,0:T(8,128)S(1)} custom-call(f32[1,128,128]{2,1,0:T(8,128)S(1)} %get-tuple-element.71), custom_call_target="InvertDiagBlocksLowerTriangular" | custom-call | tf_op jit(solution)/shard_map/jit(cholesky)/cholesky | solution.py:68
  524.5 12.1 %cholesky.487 = f32[128,128]{1,0:T(8,128)S(1)} custom-call(f32[128,128]{1,0:T(8,128)S(1)} %cholesky.594), custom_call_target="Cholesky" | custom-call | tf_op jit(solution)/shard_map/jit(cholesky)/cholesky | solution.py:68
  538.0 9.8 %custom-call.65 = f32[1,128,128]{1,2,0:T(8,128)S(1)} custom-call(f32[1,128,128]{2,1,0:T(8,128)S(1)} %get-tuple-element.68), custom_call_target="InvertDiagBlocksLowerTriangular" | custom-call | tf_op jit(solution)/shard_map/jit(cholesky)/cholesky | solution.py:68
  551.2 11.7 %cholesky.506 = f32[128,128]{1,0:T(8,128)S(1)} custom-call(f32[128,128]{1,0:T(8,128)S(1)} %cholesky.599), custom_call_target="Cholesky" | custom-call | tf_op jit(solution)/shard_map/jit(cholesky)/cholesky | solution.py:68
  564.2 10.0 %custom-call.66 = f32[1,128,128]{1,2,0:T(8,128)S(1)} custom-call(f32[1,128,128]{2,1,0:T(8,128)S(1)} %get-tuple-element.65), custom_call_target="InvertDiagBlocksLowerTriangular" | custom-call | tf_op jit(solution)/shard_map/jit(cholesky)/cholesky | solution.py:68
  577.5 11.7 %cholesky.526 = f32[128,128]{1,0:T(8,128)S(1)} custom-call(f32[128,128]{1,0:T(8,128)S(1)} %cholesky.604), custom_call_target="Cholesky" | custom-call | tf_op jit(solution)/shard_map/jit(cholesky)/cholesky | solution.py:68
  590.5 9.8 %custom-call.67 = f32[1,128,128]{1,2,0:T(8,128)S(1)} custom-call(f32[1,128,128]{2,1,0:T(8,128)S(1)} %get-tuple-element.62), custom_call_target="InvertDiagBlocksLowerTriangular" | custom-call | tf_op jit(solution)/shard_map/jit(cholesky)/cholesky | solution.py:68
  603.3 11.9 %cholesky.546 = f32[128,128]{1,0:T(8,128)S(1)} custom-call(f32[128,128]{1,0:T(8,128)S(1)} %cholesky.609), custom_call_target="Cholesky" | custom-call | tf_op jit(solution)/shard_map/jit(cholesky)/cholesky | solution.py:68
  616.6 9.8 %custom-call.68 = f32[1,128,128]{1,2,0:T(8,128)S(1)} custom-call(f32[1,128,128]{2,1,0:T(8,128)S(1)} %get-tuple-element.59), custom_call_target="InvertDiagBlocksLowerTriangular" | custom-call | tf_op jit(solution)/shard_map/jit(cholesky)/cholesky | solution.py:68
  629.0 11.7 %cholesky.564 = f32[128,128]{1,0:T(8,128)S(1)} custom-call(f32[128,128]{1,0:T(8,128)S(1)} %convolution_subtract_fusion.11), custom_call_target="Cholesky" | custom-call | tf_op jit(solution)/shard_map/jit(cholesky)/cholesky | solution.py:68
  652.7 22.8 %while.1 = (s32[]{:T(128)}, f32[1024,1024]{1,0:T(8,128)}, s32[8,2]{0,1:T(2,128)S(1)}, f32[8,128,128]{2,1,0:T(8,128)S(1)}, s32[]{:T(128)}) while((s32[]{:T(128)}, f32[1024,1024]{1,0:T(8,128)}, s32[8,2]{0,1:T(2,128)S(1)}, f32[8,128,128]{2,1,0:T(8,128)S(1)}, s32[]{:T(128)}) %tuple.61), condition=%wide.while_cond, body=%wide.while_body.sunk | while | flops 2 | bytes 131181 | solution.py:69
  675.5 79.0 %custom-call.69 = f32[8,128,128]{1,2,0:T(8,128)S(1)} custom-call(f32[8,128,128]{2,1,0:T(8,128)S(1)} %get-tuple-element.12), custom_call_target="InvertDiagBlocksLowerTriangular" | custom-call | tf_op jit(solution)/shard_map/triangular_solve | solution.py:69
  (155 shorter events, 177.8 us)
Async XLA Ops:
  6.5 237.5 %all-gather.5.cloned.1.call-start = ((), (), s32[]{:S(2)}) async-start(), calls=%async_computation | async-start | bytes 10485760 | tf_op jit(solution)/shard_map/all_gather | solution.py:64
  7.8 10.7 %collective-permute-start = (bf16[1024,256]{1,0:T(8,128)(2,1)S(1)}, bf16[1024,256]{1,0:T(8,128)(2,1)S(1)}, u32[]{:S(2)}, u32[]{:S(2)}) collective-permute-start(bf16[1024,256]{1,0:T(8,128)(2,1)S(1)} %get-tuple-element.29), channel_id=1, source_target_pairs={{0,4},{4,8},{8,12},{12,16},{16,20},{20,24},{24,28},{28,32},{32,36}... | collective-permute-start | bytes 1572872 | tf_op jit(solution)/shard_map/ppermute | solution.py:18
  12.4 10.6 %collective-permute-start.1 = (bf16[1024,256]{1,0:T(8,128)(2,1)S(1)}, bf16[1024,256]{1,0:T(8,128)(2,1)}, u32[]{:S(2)}, u32[]{:S(2)}) collective-permute-start(bf16[1024,256]{1,0:T(8,128)(2,1)S(1)} %get-tuple-element.30), channel_id=1, source_target_pairs={{4,0},{8,4},{12,8},{16,12},{20,16},{24,20},{28,24},{32,28},{36,32}... | collective-permute-start | bytes 1572872 | tf_op jit(solution)/shard_map/ppermute | solution.py:19
  18.5 0.8 copy-start.12
  32.7 7.5 copy-start.7
  40.3 2.0 copy-start
  42.4 8.0 %collective-permute-start.2 = (bf16[1024,256]{1,0:T(8,128)(2,1)S(1)}, bf16[1024,256]{1,0:T(8,128)(2,1)S(1)}, u32[]{:S(2)}, u32[]{:S(2)}) collective-permute-start(bf16[1024,256]{1,0:T(8,128)(2,1)S(1)} %get-tuple-element.27), channel_id=1, source_target_pairs={{0,4},{4,8},{8,12},{12,16},{16,20},{20,24},{24,28},{28,32},{32,36}... | collective-permute-start | bytes 1572872 | tf_op jit(solution)/shard_map/ppermute | solution.py:18
  44.3 10.5 %collective-permute-start.3 = (bf16[1024,256]{1,0:T(8,128)(2,1)S(1)}, bf16[1024,256]{1,0:T(8,128)(2,1)S(1)}, u32[]{:S(2)}, u32[]{:S(2)}) collective-permute-start(bf16[1024,256]{1,0:T(8,128)(2,1)S(1)} %get-tuple-element.28), channel_id=1, source_target_pairs={{4,0},{8,4},{12,8},{16,12},{20,16},{24,20},{28,24},{32,28},{36,32}... | collective-permute-start | bytes 1572872 | tf_op jit(solution)/shard_map/ppermute | solution.py:19
  66.2 7.5 copy-start.1
  73.7 2.1 copy-start.4
  75.9 8.0 %collective-permute-start.4 = (bf16[1024,256]{1,0:T(8,128)(2,1)S(1)}, bf16[1024,256]{1,0:T(8,128)(2,1)S(1)}, u32[]{:S(2)}, u32[]{:S(2)}) collective-permute-start(bf16[1024,256]{1,0:T(8,128)(2,1)S(1)} %get-tuple-element.25), channel_id=1, source_target_pairs={{0,4},{4,8},{8,12},{12,16},{16,20},{20,24},{24,28},{28,32},{32,36}... | collective-permute-start | bytes 1572872 | tf_op jit(solution)/shard_map/ppermute | solution.py:18
  77.8 10.5 %collective-permute-start.5 = (bf16[1024,256]{1,0:T(8,128)(2,1)S(1)}, bf16[1024,256]{1,0:T(8,128)(2,1)S(1)}, u32[]{:S(2)}, u32[]{:S(2)}) collective-permute-start(bf16[1024,256]{1,0:T(8,128)(2,1)S(1)} %get-tuple-element.26), channel_id=1, source_target_pairs={{4,0},{8,4},{12,8},{16,12},{20,16},{24,20},{28,24},{32,28},{36,32}... | collective-permute-start | bytes 1572872 | tf_op jit(solution)/shard_map/ppermute | solution.py:19
  99.6 7.5 copy-start.2
  99.6 8.0 %copy-start.5 = (f32[32,256,128,1]{1,2,3,0:T(8,128)S(1)}, f32[32,256,128,1]{1,2,3,0:T(8,128)}, u32[]{:S(2)}) copy-start(f32[32,256,128,1]{1,2,3,0:T(8,128)} %copy-done.4) | copy-start | bytes 12582916
  107.6 2.6 copy-start.8
  110.3 8.0 %collective-permute-start.6 = (bf16[1024,256]{1,0:T(8,128)(2,1)S(1)}, bf16[1024,256]{1,0:T(8,128)(2,1)S(1)}, u32[]{:S(2)}, u32[]{:S(2)}) collective-permute-start(bf16[1024,256]{1,0:T(8,128)(2,1)S(1)} %get-tuple-element.23), channel_id=1, source_target_pairs={{0,4},{4,8},{8,12},{12,16},{16,20},{20,24},{24,28},{28,32},{32,36}... | collective-permute-start | bytes 1572872 | tf_op jit(solution)/shard_map/ppermute | solution.py:18
  112.2 12.2 %collective-permute-start.7 = (bf16[1024,256]{1,0:T(8,128)(2,1)S(1)}, bf16[1024,256]{1,0:T(8,128)(2,1)S(1)}, u32[]{:S(2)}, u32[]{:S(2)}) collective-permute-start(bf16[1024,256]{1,0:T(8,128)(2,1)S(1)} %get-tuple-element.24), channel_id=1, source_target_pairs={{4,0},{8,4},{12,8},{16,12},{20,16},{24,20},{28,24},{32,28},{36,32}... | collective-permute-start | bytes 1572872 | tf_op jit(solution)/shard_map/ppermute | solution.py:19
  135.7 7.5 copy-start.3
  135.7 8.0 %copy-start.6 = (f32[32,256,128,1]{1,2,3,0:T(8,128)S(1)}, f32[32,256,128,1]{1,2,3,0:T(8,128)}, u32[]{:S(2)}) copy-start(f32[32,256,128,1]{1,2,3,0:T(8,128)} %copy-done.4) | copy-start | bytes 12582916
  135.7 9.2 %copy-start.9 = (f32[32,256,128,1]{1,2,3,0:T(8,128)S(1)}, f32[32,256,128,1]{1,2,3,0:T(8,128)}, u32[]{:S(2)}) copy-start(f32[32,256,128,1]{1,2,3,0:T(8,128)} %copy-done.8) | copy-start | bytes 12582916
  149.3 217.9 %all-gather.9.cloned.1.call-start = ((), (), s32[]{:S(2)}) async-start(), calls=%async_computation.2 | async-start | bytes 34603008 | tf_op jit(solution)/shard_map/all_gather | solution.py:66
  251.4 176.2 %all-gather.7.cloned.1.call-start = ((), (), s32[]{:S(2)}) async-start(), calls=%async_computation.1 | async-start | bytes 5242880 | tf_op jit(solution)/shard_map/all_gather | solution.py:67
  442.6 2.0 copy-start.11
  754.5 3.2 copy-start.10
  765.9 11.2 %slice-start = ((s8[8388608]{0:T(1024)(128)(4,1)}), s8[4194304]{0:T(1024)(128)(4,1)S(1)}, s32[]{:S(2)}) async-start(s8[8388608]{0:T(1024)(128)(4,1)} %bitcast.198), calls=%async_computation.3 | async-start | bytes 8388608
  769.4 7.7 slice-start.1
Sparse Core Ops, SparseCore 0:
  149.5 94.5 all-gather.4
  251.5 115.6 all-gather.8
  380.5 46.9 all-gather.6
